TPU v7x, 256 devices: a whole 4x4x8 slice. The times are simulated.
256 devices in a mesh: dp: 8 (over z_lo, y), seq: 32 (over z_hi, x, core).
Axes of the slice: x: 4, y: 4, z: 8 (z_hi: 4, z_lo: 2; z = z_hi * 2 + z_lo), core: 2. Of those that a mesh axis runs over, the one named last changes fastest.
Arguments:
- queries: bfloat16 [32768, 4096], P(('dp', 'seq')), may hold values from -64 to 64
- keys: bfloat16 [32768, 4096], P(('dp', 'seq')), may hold values from -64 to 64
- values: bfloat16 [32768, 4096], P(('dp', 'seq')), may hold values from -6 to 6
- out_grad: bfloat16 [32768, 4096], P(('dp', 'seq')), may hold values from -6 to 6
- gain_q: float32 [32, 128], P('seq', 'dp'), may hold values from 0.5 to 10
- gain_k: float32 [32, 128], P('seq', 'dp'), may hold values from 0.5 to 10
- clip_ids: int32 [8, 4096], P('dp', 'seq'), may hold values from 0 to 31, never falling along the last dimension, each value on 1 to 256 neighbouring positions
- counts: int32 [8, 32], P('dp', 'seq'), may hold values from 42 to 128, as said below
Outputs:
- grad_queries: bfloat16 [32768, 4096], P(('dp', 'seq'))
- grad_keys: bfloat16 [32768, 4096], P(('dp', 'seq'))
- grad_values: bfloat16 [32768, 4096], P(('dp', 'seq'))
- grad_gain_q: float32 [32, 128], P('seq')
- grad_gain_k: float32 [32, 128], P('seq')
Inputs may be any that keep to these rules, and one draw needn't show every extreme that they name: `counts`: in every row one device holds 128 live slots and another a third of 128, rounded down. `clip_ids`: along a row clip numbers never fall; each clip takes 1 to 256 consecutive slots, one exactly 256.
All inputs are finite; a program needn't handle non-finite values.
Results may differ from a plain program's by a relative error of at most 0.011.
The roundings to bfloat16 on the way count: a program that leaves them out, or rounds other values in their place, can miss the bound.
Values may be sent and summed in bfloat16 or wider, within the bound.
No kernel may reach another device: no remote copies, remote signals or barrier semaphores. Data moves between devices by JAX's collectives and lax.ppermute only.
A program may use at most 192 MiB of HBM per device.

v0:
```python
import functools

import jax
import jax.numpy as jnp
from jax import lax
from jax.experimental import pallas as pl
from jax.experimental.pallas import tpu as pltpu
from jax.sharding import PartitionSpec as P

EPS = 1e-06
NEG = -1e30
HD = 128
ROWS = 128
PAIR = 256
HEADS = 16
ALIGN = 16
LINE = 4
CAP = 1152
PARTS = (CAP // 2,) * 2
FIRST = 768
REST = CAP - FIRST
SENT = len(PARTS) + 2
PADDED = CAP + PAIR
SCALE = HD**-0.5
LOG2E = 1.4426950408889634
BF = jnp.bfloat16
F32 = jnp.float32
CORE, CHIP, A_L, B_L, A_R, B_R, N_L, N_R, PA_L, PB_L, PA_R, PB_R = range(12)
KNOWN = 5
ANYWHERE = pl.BlockSpec(memory_space=pl.ANY)
IN_VMEM = pl.BlockSpec(memory_space=pltpu.VMEM)
IN_SMEM = pl.BlockSpec(memory_space=pltpu.SMEM)


def aligned(index):
    return pl.multiple_of(index, ALIGN)


def lanes(position):
    return pl.ds(pl.multiple_of(position * HD, HD), HD)


def params(mib):
    return pltpu.CompilerParams(vmem_limit_bytes=mib * 1024 * 1024)


def whole(shape):
    return pl.BlockSpec(shape, lambda j, m: (0,) * len(shape))


def run_copies(copies):
    for copy in copies:
        copy.start()
    for copy in copies:
        copy.wait()


def rows_of(held, start, length):
    return held.at[:, pl.ds(start, length), :]


def pick_kernel(
    place, q_ref, k_ref, v_ref, d_ref, gain_cols, info, info_other, out_ref, known_ref, row
):
    other = 1 - place[CORE]

    @pl.when(pl.program_id(0) == 0)
    def _():
        width = gain_cols.shape[2]
        row[...] = jnp.zeros_like(row)
        for n in range(gain_cols.shape[0]):
            row[0:2, n * width : (n + 1) * width] = gain_cols[n]
        row[2:3, :] = info[0:1, :]
        row[3:4, :] = info_other[0:1, :]
        row[4:5, 0:1] = info[1:2, 0:1]
        row[4:5, 1:2] = info_other[1:2, 0:1]
        known_ref[...] = jnp.broadcast_to(row[0:KNOWN, :][None], known_ref.shape)

    for t, ref in enumerate((q_ref, k_ref, v_ref, d_ref)):
        for i in range(out_ref.shape[2] // HD):
            out_ref[t, :, i * HD : (i + 1) * HD] = ref[:, lanes(2 * i + other)]


def pick_other(place, tensors, gain_cols, info, info_other, per=8):
    known = jax.ShapeDtypeStruct((HEADS, KNOWN, HD), F32)
    small = (gain_cols, info, info_other)
    return pl.pallas_call(
        pick_kernel,
        out_shape=(jax.ShapeDtypeStruct((4, ROWS, HEADS * HD), BF), known),
        grid_spec=pltpu.PrefetchScalarGridSpec(
            num_scalar_prefetch=1,
            grid=(HEADS // per,),
            in_specs=own_specs(per)[:4] + [whole(array.shape) for array in small],
            out_specs=(own_specs(per)[4], whole(known.shape)),
            scratch_shapes=[pltpu.VMEM((8, HD), F32)],
        ),
        compiler_params=params(12),
    )(place, *tensors, *small)


def chip_halves(info, core):
    ids, counts = (info[0:1], info[1:2]), (info[2:3, 0:1], info[2:3, 1:2])

    def ordered(mine, other):
        return jnp.where(core == 0, mine, other), jnp.where(core == 0, other, mine)

    return ordered(*ids), ordered(*counts)


def count_equal(halves, wanted):
    hits = [jnp.where(half == wanted, 1.0, 0.0).astype(F32) for half in halves]
    return jnp.sum(hits[0] + hits[1]).astype(jnp.int32)


def edge_split(long_a, long_b, left_chip):
    blocks_a = lax.div(long_a + ALIGN - 1, ALIGN)
    blocks_b = lax.div(long_b + ALIGN - 1, ALIGN)
    least = HEADS - lax.div(CAP // ALIGN, jnp.maximum(blocks_a, 1))
    most = lax.div(CAP // ALIGN, jnp.maximum(blocks_b, 1))
    spot = lax.rem(left_chip, LINE)
    wanted = jnp.where(spot == 0, 0, jnp.where(spot == LINE - 2, HEADS, HEADS // 2))
    to_left = jnp.minimum(jnp.maximum(wanted, least), most)
    return blocks_a * ALIGN, blocks_b * ALIGN, to_left


def chip_infos(table, chip):
    spots = (chip, jnp.maximum(chip - 1, 0), jnp.minimum(chip + 1, HEADS - 1))
    return [table[spot][2:KNOWN] for spot in spots]


def write_plan(place, table, meta):
    core, chip = place[CORE], place[CHIP]
    infos = chip_infos(table, chip)
    own, _ = chip_halves(infos[0], core)
    left, _ = chip_halves(infos[1], core)
    right, _ = chip_halves(infos[2], core)
    left_last, own_first = jnp.max(left[1]), jnp.min(own[0])
    own_last, right_first = jnp.max(own[1]), jnp.min(right[0])
    cross_l = (chip > 0) & (left_last == own_first)
    cross_r = (chip < HEADS - 1) & (right_first == own_last)
    a_l = jnp.where(cross_l, count_equal(left, left_last), 0)
    b_l = jnp.where(cross_l, count_equal(own, own_first), 0)
    a_r = jnp.where(cross_r, count_equal(own, own_last), 0)
    b_r = jnp.where(cross_r, count_equal(right, right_first), 0)
    pa_l, pb_l, n_l = edge_split(a_l, b_l, jnp.maximum(chip - 1, 0))
    pa_r, pb_r, n_r = edge_split(a_r, b_r, chip)
    n_l = jnp.where(cross_l, n_l, HEADS)
    n_r = jnp.where(cross_r, n_r, 0)
    values = [core, chip, a_l, b_l, a_r, b_r, n_l, n_r, pa_l, pb_l, pa_r, pb_r]
    for n, value in enumerate(values):
        meta[n] = value


def even(meta):
    return lax.rem(meta[CHIP], 2) == 0


def at_corner(meta):
    place = lax.rem(meta[CHIP], LINE)
    return (place == 0) | (place == LINE - 1)


def cut(table, *lengths):
    starts = [sum(lengths[:n]) for n in range(len(lengths))]
    return [table.at[:, pl.ds(a, n), :] for a, n in zip(starts, lengths, strict=True)]


def copies_of(sources, targets, sems):
    return [
        pltpu.make_async_copy(a, b, sems.at[n])
        for n, (a, b) in enumerate(zip(sources, targets, strict=True))
    ]


def start_one(cases):
    for wanted, copies in cases:

        @pl.when(wanted)
        def _():
            for copy in copies:
                copy.start()

    return cases[0][1]


def wait_all(copies):
    for copy in copies:
        copy.wait()


def send_pieces(meta, left, right, pieces, sems):
    def pieces_of(a, b):
        return copies_of(cut(a, *PARTS) + cut(b, FIRST, REST), pieces, sems)

    is_even = even(meta)
    wait_all(
        start_one(
            [
                (is_even, pieces_of(right, left)),
                (jnp.logical_not(is_even), pieces_of(left, right)),
            ]
        )
    )


def load_both(meta, pieces, held_left, held_right, sems):
    *direct, rest, relayed = pieces

    def pieces_of(a, b, last):
        return copies_of([*direct, last], cut(a, *PARTS) + cut(b, FIRST, REST), sems)

    is_even, corner = even(meta), at_corner(meta)
    is_odd, inner = jnp.logical_not(is_even), jnp.logical_not(corner)
    return start_one(
        [
            (is_even & corner, pieces_of(held_right, held_left, relayed)),
            (is_even & inner, pieces_of(held_right, held_left, rest)),
            (is_odd & corner, pieces_of(held_left, held_right, relayed)),
            (is_odd & inner, pieces_of(held_left, held_right, rest)),
        ]
    )


def half_rows(half):
    return pl.ds(pl.multiple_of(half * ROWS, ROWS), ROWS)


def fill_windows(win, core, own_refs, rec_ref):
    for i in range(win.shape[0]):
        for t, ref in enumerate(own_refs):
            win[i, t, half_rows(core), :] = ref[:, lanes(2 * i + core)]
            win[i, t, half_rows(1 - core), :] = rec_ref[t, :, i * HD : (i + 1) * HD]


def pack_kernel(place, q_ref, k_ref, v_ref, d_ref, rec_ref, table, meta, *refs):
    *pieces, win, left_ref, right_ref, sems = refs
    per = rec_ref.shape[2] // HD
    core = place[CORE]
    step = pl.program_id(0)

    @pl.when(step == 0)
    def _():
        write_plan(place, table, meta)

    fill_windows(win, core, (q_ref, k_ref, v_ref, d_ref), rec_ref)
    for i in range(per):
        head = step * per + i

        @pl.when(head < meta[N_L])
        def _():
            for t in range(4):
                left_ref[t, pl.ds(aligned(head * meta[PB_L]), PAIR), :] = win[i, t]

        @pl.when(head >= meta[N_R])
        def _():
            for t in range(4):
                right_ref[t, pl.ds(aligned((HEADS - head) * meta[PA_R]), PAIR), :] = win[i, t]

    @pl.when(step == pl.num_programs(0) - 1)
    def _():
        send_pieces(
            meta,
            rows_of(left_ref, 0, CAP),
            rows_of(right_ref, PAIR, CAP),
            pieces,
            sems,
        )


def own_specs(per):
    return [pl.BlockSpec((ROWS, 2 * per * HD), lambda j, m: (0, j))] * 4 + [
        pl.BlockSpec((4, ROWS, per * HD), lambda j, m: (0, 0, j))
    ]


def pieces_shape(tensors):
    return [jax.ShapeDtypeStruct((tensors, n, HD), BF) for n in (*PARTS, FIRST, REST)]


def pack_halos(place, tensors, rec, table, per=8):
    return pl.pallas_call(
        pack_kernel,
        out_shape=(
            jax.ShapeDtypeStruct((16,), jnp.int32),
            *pieces_shape(4),
        ),
        grid_spec=pltpu.PrefetchScalarGridSpec(
            num_scalar_prefetch=1,
            grid=(HEADS // per,),
            in_specs=own_specs(per) + [whole(table.shape)],
            out_specs=(IN_SMEM, *([ANYWHERE] * SENT)),
            scratch_shapes=[
                pltpu.VMEM((per, 4, PAIR, HD), BF),
                pltpu.VMEM((4, PADDED, HD), BF),
                pltpu.VMEM((4, PADDED, HD), BF),
                pltpu.SemaphoreType.DMA((SENT,)),
            ],
        ),
        compiler_params=params(16),
    )(place, *tensors, rec, table)


def matmul(a, b, contract_a, contract_b):
    return lax.dot_general(
        a, b, (((contract_a,), (contract_b,)), ((), ())), preferred_element_type=F32
    )


def norm_parts(rows, gain):
    widened = rows.astype(F32)
    scaled = lax.rsqrt(jnp.mean(widened * widened, axis=-1, keepdims=True) + EPS)
    unit_rows = widened * scaled
    return scaled, unit_rows, (unit_rows * gain).astype(BF)


def norm_back(scaled, unit_rows, gain, upper):
    terms = upper * unit_rows
    gain = gain * SCALE
    mean = jnp.mean(terms * gain, axis=-1, keepdims=True)
    grad = scaled * (gain * upper - unit_rows * mean)
    return grad.astype(BF), jnp.sum(terms, axis=0, keepdims=True) * SCALE


def solve(problems):
    each = range(len(problems))
    q_rows, k_rows, v_rows, d_rows, gain_q, gain_k, bias, q_live = zip(*problems, strict=True)
    q_parts = [norm_parts(q_rows[n], gain_q[n]) for n in each]
    k_parts = [norm_parts(k_rows[n], gain_k[n]) for n in each]
    raw = [matmul(k_parts[n][2], q_parts[n][2], 1, 1) for n in each]
    d_weights = [matmul(v_rows[n], d_rows[n], 1, 1) for n in each]
    weights = []
    for n in each:
        scores = raw[n] * (SCALE * LOG2E) + bias[n]
        exponent = jnp.exp2(scores - jnp.max(scores, axis=0, keepdims=True))
        total = jnp.sum(exponent, axis=0, keepdims=True)
        weights.append((exponent * (q_live[n] / total)).astype(BF))
    dv_rows = [matmul(weights[n], d_rows[n], 1, 0) for n in each]
    d_scores = []
    for n in each:
        wide = weights[n].astype(F32)
        row_delta = jnp.sum(wide * d_weights[n], axis=0, keepdims=True)
        d_scores.append((wide * (d_weights[n] - row_delta)).astype(BF))
    dk = [matmul(d_scores[n], q_parts[n][2], 1, 0) for n in each]
    dq = [matmul(d_scores[n], k_parts[n][2], 0, 0) for n in each]
    results = []
    for n in each:
        grad_k, gain_k_part = norm_back(k_parts[n][0], k_parts[n][1], gain_k[n], dk[n])
        grad_q, gain_q_part = norm_back(q_parts[n][0], q_parts[n][1], gain_q[n], dq[n])
        grads = (grad_q, grad_k, dv_rows[n].astype(BF))
        results.append((grads, gain_q_part, gain_k_part))
    return results


def link_codes(side, meta, table):
    core, infos = meta[CORE], chip_infos(table, meta[CHIP])
    own_ids, own_counts = chip_halves(infos[0], core)
    _, far_counts = chip_halves(infos[side], core)
    codes = []
    for half in range(2):
        lane = lax.broadcasted_iota(jnp.int32, (1, ROWS), 1)
        slot = lane + half * ROWS
        live = lane.astype(F32) < own_counts[half]
        far = lane.astype(F32) < far_counts[half]
        if side == 0:
            inside = live & (slot >= meta[B_L]) & (slot < PAIR - meta[A_R])
            code = jnp.where(inside, own_ids[half], -1.0)
        elif side == 1:
            inside = (live & (slot < meta[B_L])) | (far & (slot >= PAIR - meta[A_L]))
            code = jnp.where(inside, 0.0, -1.0)
        else:
            inside = (live & (slot >= PAIR - meta[A_R])) | (far & (slot < meta[B_R]))
            code = jnp.where(inside, 0.0, -1.0)
        codes.append(code.astype(F32))
    return codes


def fill_links(bias, q_live, codes):
    for a in range(2):
        q_live[0:1, a * ROWS : (a + 1) * ROWS] = (codes[a] >= 0.0).astype(F32)
        key_codes = jnp.broadcast_to(codes[a], (ROWS, ROWS)).T
        for b in range(2):
            linked = (key_codes == codes[b]) & (codes[b] >= 0.0)
            bias[a * ROWS : (a + 1) * ROWS, b * ROWS : (b + 1) * ROWS] = jnp.where(
                linked, 0.0, NEG
            ).astype(F32)


def mid_kernel(
    meta,
    q_ref,
    k_ref,
    v_ref,
    d_ref,
    rec_ref,
    table,
    out_ref,
    gg_ref,
    win,
    bias,
    q_live,
):
    per = rec_ref.shape[2] // HD
    core = meta[CORE]

    @pl.when(pl.program_id(0) == 0)
    def _():
        fill_links(bias, q_live, link_codes(0, meta, table))

    fill_windows(win, core, (q_ref, k_ref, v_ref, d_ref), rec_ref)
    heads = [pl.program_id(0) * per + i for i in range(per)]
    gains = [table[head] for head in heads]
    results = solve(
        [
            (*(win[i, t] for t in range(4)), gains[i][0:1], gains[i][1:2], bias[...], q_live[0:1, :])
            for i in range(per)
        ]
    )
    for i, (grads, part_q, part_k) in enumerate(results):
        for t in range(3):
            for half in range(2):
                out_ref[lax.rem(half + core, 2), t, :, i * HD : (i + 1) * HD] = grads[t][
                    half * ROWS : (half + 1) * ROWS
                ]
        gg_ref[heads[i]] = jnp.concatenate([part_q, part_k], axis=0)


def solve_mid(meta, tensors, rec, table, per=4):
    per_head = jax.ShapeDtypeStruct((HEADS, 2, HD), F32)
    return pl.pallas_call(
        mid_kernel,
        out_shape=(jax.ShapeDtypeStruct((2, 3, ROWS, HEADS * HD), BF), per_head),
        grid_spec=pltpu.PrefetchScalarGridSpec(
            num_scalar_prefetch=1,
            grid=(HEADS // per,),
            in_specs=own_specs(per) + [whole(table.shape)],
            out_specs=(half_spec(per), whole(per_head.shape)),
            scratch_shapes=[
                pltpu.VMEM((per, 4, PAIR, HD), BF),
                pltpu.VMEM((PAIR, PAIR), F32),
                pltpu.VMEM((8, PAIR), F32),
            ],
        ),
        compiler_params=params(32),
    )(meta, *tensors, rec, table)


def half_spec(per):
    return pl.BlockSpec((2, 3, ROWS, per * HD), lambda j, m: (0, 0, 0, j))


def row_numbers(rows):
    return lax.broadcasted_iota(jnp.int32, (rows, HD), 0).astype(F32).astype(BF)


def bound(value):
    return jnp.full((1, HD), value, jnp.int32).astype(F32).astype(BF)


def edge_kernel(
    meta, q_ref, k_ref, v_ref, d_ref, rec_ref, table, mid_ref, gg_mid_ref, *refs
):
    halos, (out_ref, gg_ref, *pieces) = refs[: SENT + 1], refs[SENT + 1 : -6]
    win, bias, q_live, held, back, sems = refs[-6:]
    per = rec_ref.shape[2] // HD
    core = meta[CORE]
    step = pl.program_id(0)

    @pl.when(step == 0)
    def _():
        copies = load_both(
            meta,
            halos,
            rows_of(held.at[0], PAIR, CAP),
            rows_of(held.at[1], 0, CAP),
            sems,
        )
        for side in range(2):
            fill_links(
                bias.at[side], q_live.at[side], link_codes(side + 1, meta, table)
            )
        gg_ref[...] = gg_mid_ref[...]
        for copy in copies:
            copy.wait()

    fill_windows(win, core, (q_ref, k_ref, v_ref, d_ref), rec_ref)
    out_ref[...] = mid_ref[...]
    heads = [step * per + i for i in range(per)]
    on_left = [head >= meta[N_L] for head in heads]
    on_right = [head < meta[N_R] for head in heads]
    row = row_numbers(PAIR)

    def solve_side(lefts, rights):
        problems, spots = [], []
        for i, head in enumerate(heads):
            side = jnp.where(lefts[i], 0, 1)
            use = jnp.logical_or(lefts[i], rights[i])
            at = jnp.where(lefts[i], (HEADS - head) * meta[PA_L], head * meta[PB_R])
            span = pl.ds(aligned(jnp.where(use, at, PADDED)), PAIR)
            source = pl.ds(aligned(jnp.where(use, at, 0)), PAIR)
            halo = (row >= bound(jnp.where(lefts[i], PAIR - meta[A_L], 0))) & (
                row < bound(jnp.where(lefts[i], PAIR, jnp.where(use, meta[B_R], 0)))
            )
            local = (row >= bound(jnp.where(lefts[i], 0, PAIR - meta[A_R]))) & (
                row < bound(jnp.where(lefts[i], meta[B_L], jnp.where(use, PAIR, 0)))
            )
            window = [jnp.where(halo, held[side, t, source, :], win[i, t]) for t in range(4)]
            gains = table[head]
            problems.append((*window, gains[0:1], gains[1:2], bias[side], q_live[side, 0:1, :]))
            spots.append((side, span, local, use.astype(F32)))
        for i, (grads, part_q, part_k) in enumerate(solve(problems)):
            side, span, local, counts = spots[i]
            cols = slice(i * HD, (i + 1) * HD)
            for t in range(3):
                back[side, t, span, :] = grads[t]
                for half in range(2):
                    rows = slice(half * ROWS, (half + 1) * ROWS)
                    place = lax.rem(half + core, 2)
                    out_ref[place, t, :, cols] = jnp.where(
                        local[rows], grads[t][rows], out_ref[place, t, :, cols]
                    )
            gg_ref[heads[i]] += jnp.concatenate([part_q, part_k], axis=0) * counts

    def some(flags):
        return functools.reduce(jnp.logical_or, flags)

    @pl.when(some(on_left + on_right))
    def _():
        solve_side(on_left, on_right)

    both = [jnp.logical_and(*pair) for pair in zip(on_left, on_right, strict=True)]

    @pl.when(some(both))
    def _():
        solve_side([jnp.logical_and(flag, jnp.logical_not(flag)) for flag in both], both)

    @pl.when(step == pl.num_programs(0) - 1)
    def _():
        send_pieces(
            meta,
            rows_of(back.at[0], PAIR, CAP),
            rows_of(back.at[1], 0, CAP),
            pieces,
            sems,
        )


def solve_edges(meta, tensors, rec, table, mid, gg_mid, halos, per=4):
    return pl.pallas_call(
        edge_kernel,
        out_shape=(
            jax.ShapeDtypeStruct(mid.shape, BF),
            jax.ShapeDtypeStruct(gg_mid.shape, F32),
            *pieces_shape(3),
        ),
        grid_spec=pltpu.PrefetchScalarGridSpec(
            num_scalar_prefetch=1,
            grid=(HEADS // per,),
            in_specs=own_specs(per)
            + [whole(table.shape), half_spec(per), whole(gg_mid.shape)]
            + [ANYWHERE] * (SENT + 1),
            out_specs=(half_spec(per), whole(gg_mid.shape), *([ANYWHERE] * SENT)),
            scratch_shapes=[
                pltpu.VMEM((per, 4, PAIR, HD), BF),
                pltpu.VMEM((2, PAIR, PAIR), F32),
                pltpu.VMEM((2, 8, PAIR), F32),
                pltpu.VMEM((2, 4, PADDED, HD), BF),
                pltpu.VMEM((2, 3, PADDED + PAIR, HD), BF),
                pltpu.SemaphoreType.DMA((SENT,)),
            ],
        ),
        compiler_params=params(40),
    )(meta, *tensors, rec, table, mid, gg_mid, *halos)


def load_returned(meta, pieces, held_left, held_right, sems):
    for copy in load_both(
        meta, pieces, rows_of(held_left, 0, CAP), rows_of(held_right, PAIR, CAP), sems
    ):
        copy.wait()


def merged(meta, head, half, rows, held_left, held_right):
    use_left = head < meta[N_L]
    use_right = head >= meta[N_R]
    base = half * ROWS
    left_at = jnp.where(use_left, head * meta[PB_L], 0) + base
    right_at = jnp.where(use_right, (HEADS - head) * meta[PA_R], 0) + base
    row = row_numbers(ROWS)
    at_head = row < bound(jnp.where(use_left, meta[B_L], 0) - base)
    at_tail = row >= bound(jnp.where(use_right, PAIR - meta[A_R], PAIR) - base)
    done = []
    for t, part in enumerate(rows):
        part = jnp.where(at_head, held_left[t, pl.ds(aligned(left_at), ROWS), :], part)
        part = jnp.where(at_tail, held_right[t, pl.ds(aligned(right_at), ROWS), :], part)
        done.append(part)
    return done


def merge_kernel(meta, in_ref, *refs):
    pieces, (_, send_ref, held_left, held_right, sems) = refs[: SENT + 1], refs[SENT + 1 :]
    per = in_ref.shape[3] // HD
    step = pl.program_id(0)

    @pl.when(step == 0)
    def _():
        load_returned(meta, pieces, held_left, held_right, sems)

    for i in range(per):
        cols = slice(i * HD, (i + 1) * HD)
        rows = [in_ref[0, t, :, cols] for t in range(3)]
        rows = merged(meta, step * per + i, 1 - meta[CORE], rows, held_left, held_right)
        for t in range(3):
            send_ref[t, :, cols] = rows[t]


def held_scratch():
    return [
        pltpu.VMEM((3, PADDED, HD), BF),
        pltpu.VMEM((3, PADDED, HD), BF),
        pltpu.SemaphoreType.DMA((SENT,)),
    ]


def merge_other(meta, own, returned, after, per=8):
    return pl.pallas_call(
        merge_kernel,
        out_shape=jax.ShapeDtypeStruct((3, ROWS, HEADS * HD), BF),
        grid_spec=pltpu.PrefetchScalarGridSpec(
            num_scalar_prefetch=1,
            grid=(HEADS // per,),
            in_specs=[pl.BlockSpec((1, 3, ROWS, per * HD), lambda j, m: (1, 0, 0, j))]
            + [ANYWHERE] * (SENT + 2),
            out_specs=pl.BlockSpec((3, ROWS, per * HD), lambda j, m: (0, 0, j)),
            scratch_shapes=held_scratch(),
        ),
        compiler_params=params(16),
    )(meta, own, *returned, after)


def weave_kernel(meta, in_ref, rec_ref, *refs):
    pieces, (gg_parts, *outs, gg_q, gg_k, held_left, held_right, sems) = refs[: SENT + 1], refs[SENT + 1 :]
    per = in_ref.shape[3] // HD
    core = meta[CORE]
    step = pl.program_id(0)

    @pl.when(step == 0)
    def _():
        load_returned(meta, pieces, held_left, held_right, sems)
        total = jnp.sum(gg_parts[...], axis=0)
        gg_q[...] = total[0:1]
        gg_k[...] = total[1:2]

    for i in range(per):
        cols = slice(i * HD, (i + 1) * HD)
        rows = [in_ref[0, t, :, cols] for t in range(3)]
        rows = merged(meta, step * per + i, core, rows, held_left, held_right)
        for t in range(3):
            outs[t][:, lanes(2 * i + core)] = rows[t]
            outs[t][:, lanes(2 * i + 1 - core)] = rec_ref[t, :, cols]


def weave(meta, own, rec, returned, gg_parts, per=8):
    return pl.pallas_call(
        weave_kernel,
        out_shape=(jax.ShapeDtypeStruct((ROWS, 2 * HEADS * HD), BF),) * 3
        + (jax.ShapeDtypeStruct((1, HD), F32),) * 2,
        grid_spec=pltpu.PrefetchScalarGridSpec(
            num_scalar_prefetch=1,
            grid=(HEADS // per,),
            in_specs=[
                pl.BlockSpec((1, 3, ROWS, per * HD), lambda j, m: (0, 0, 0, j)),
                pl.BlockSpec((3, ROWS, per * HD), lambda j, m: (0, 0, j)),
            ]
            + [ANYWHERE] * (SENT + 1)
            + [whole(gg_parts.shape)],
            out_specs=(pl.BlockSpec((ROWS, 2 * per * HD), lambda j, m: (0, j)),) * 3
            + (whole((1, HD)),) * 2,
            scratch_shapes=held_scratch(),
        ),
        compiler_params=params(16),
    )(meta, own, rec, *returned, gg_parts)


def exchange(pieces, size):
    *straight, first, rest = pieces
    line = 2 * LINE
    wrap = line - 2
    steps = [(i, i + 2) for i in range(size - 2)]
    evens = [pair for pair in steps if pair[0] // 2 % 2 == 0]
    odds = [pair for pair in steps if pair[0] // 2 % 2 == 1]
    turns = [pair for pair in odds if pair[0] % line >= wrap]
    inner = [pair for pair in odds if pair[0] % line < wrap]

    def both(pairs):
        return pairs + [(j, i) for i, j in pairs]

    def move(array, pairs):
        return lax.ppermute(array, "seq", pairs)

    along_x = [(i, i - wrap) for i, _ in turns] + [(j, j + wrap) for _, j in turns]
    along_z = [(i - wrap, j) for i, j in turns] + [(j + wrap, i) for i, j in turns]
    hop = move(rest, both(inner) + along_x)
    from_first = move(first, both(odds))
    from_even = [move(piece, both(evens)) for piece in straight]
    return (*from_even, from_first, hop, move(hop, along_z))


def shards(queries, keys, values, out_grad, gain_q, gain_k, clip_ids, counts):
    size = lax.axis_size("seq")
    groups = lax.axis_size("dp")
    chips = size // 2
    seq = lax.axis_index("seq")
    swap = [(i, i ^ 1) for i in range(size)]
    place = jnp.stack([seq % 2, seq // 2]).astype(jnp.int32)
    tensors = tuple(
        pltpu.with_memory_space_constraint(t, pltpu.HBM)
        for t in (queries, keys, values, out_grad)
    )

    same_core = [list(range(core, size, 2)) for core in range(2)]
    same_cores = [
        [d * size + at for d in range(groups) for at in one_core] for one_core in same_core
    ]

    def all_to_all(array, axis, among=None):
        return lax.all_to_all(array, axis, 0, 0, axis_index_groups=among, tiled=True)

    info = jnp.concatenate([clip_ids, jnp.broadcast_to(counts, (1, ROWS))], axis=0).astype(F32)
    info_other = lax.ppermute(info, "seq", swap)
    gain_own = jnp.concatenate([gain_q, gain_k], axis=0)
    gain_cols = all_to_all(jnp.broadcast_to(gain_own[None], (groups,) + gain_own.shape), "dp")
    picked, known = pick_other(place, tensors, gain_cols, info, info_other)
    rec = lax.ppermute(picked, "seq", swap)
    table = all_to_all(known, "seq", same_core)

    meta, *pieces = pack_halos(place, tensors, rec, table)
    halos = exchange(pieces, size)
    mid, gg_mid = solve_mid(meta, tensors, rec, table)
    own, gg, *pieces = solve_edges(meta, tensors, rec, table, mid, gg_mid, halos)
    returned = exchange(pieces, size)
    gg_parts = all_to_all(
        jnp.broadcast_to(gg[None], (groups,) + gg.shape).reshape(groups * chips, 2, HD),
        ("dp", "seq"),
        same_cores,
    )
    send = merge_other(meta, own, returned, gg_parts)
    other = lax.ppermute(send, "seq", swap)
    return tuple(weave(meta, own, other, returned, gg_parts))


def solution(mesh):
    rows = P(("dp", "seq"), None)
    cells = P("seq", "dp")
    slots = P("dp", "seq")
    return jax.shard_map(
        shards,
        mesh=mesh,
        in_specs=(rows, rows, rows, rows, cells, cells, slots, slots),
        out_specs=(rows, rows, rows, P("seq", None), P("seq", None)),
        check_vma=False,
    )
```

profile of v0, /device:TPU:1, one launch (start us, length us, event | category | flops | bytes accessed | tf_op | source)
XLA Modules:
  0.0 150.6 jit_solution(1673688287287480825)
XLA Ops:
  0.6 0.7 pad_maximum_fusion
  1.3 0.6 broadcast_in_dim.6
  1.9 6.4 %all-to-all-start = ((f32[8,2,16]{2,1,0:T(2,128)}), f32[8,2,16]{2,1,0:T(2,128)S(1)}, u32[]{:S(2)}, u32[]{:S(2)}) async-start(f32[8,2,16]{2,1,0:T(2,128)} %broadcast_in_dim.6), calls=%async_computation | async-start | bytes 16384 | tf_op jit(solution)/shard_map/all_to_all | solution.py:726
  8.9 0.7 pad_convert_fusion.info
  9.6 1.0 collective-permute-start
  10.6 0.1 pad_add_fusion.place
  10.6 0.7 collective-permute-done.info_other
  11.4 1.9 %all-to-all-done.gain_cols = f32[8,2,16]{2,1,0:T(2,128)S(1)} async-done(((f32[8,2,16]{2,1,0:T(2,128)}), f32[8,2,16]{2,1,0:T(2,128)S(1)}, u32[]{:S(2)}, u32[]{:S(2)}) %all-to-all-start) | async-done | bytes 1056 | tf_op jit(solution)/shard_map/all_to_all | solution.py:726
  13.3 3.1 %shard_map.119 = (bf16[4,128,2048]{2,1,0:T(8,128)(2,1)S(1)}, f32[16,5,128]{2,1,0:T(8,128)S(1)}) custom-call(s32[2]{0:T(128)S(1)} %pad_add_fusion.place, bf16[128,4096]{1,0:T(8,128)(2,1)} %q_ref.7, bf16[128,4096]{1,0:T(8,128)(2,1)} %k_ref.7, bf16[128,4096]{1,0:T(8,128)(2,1)} %v_ref.7, bf16[128,4096]{1,0:T(8,128)(2,1)} %d_ref.7, ...), custom_call_target="tpu_custom_call" | custom-call | tf_op jit(solution)/shard_map/pallas_call | solution.py:87
  16.4 2.2 %collective-permute-start.1 = (bf16[4,128,2048]{2,1,0:T(8,128)(2,1)S(1)}, bf16[4,128,2048]{2,1,0:T(8,128)(2,1)S(1)}, u32[]{:S(2)}, u32[]{:S(2)}) collective-permute-start(bf16[4,128,2048]{2,1,0:T(8,128)(2,1)S(1)} %get-tuple-element.20), channel_id=1, source_target_pairs={{0,1},{1,0},{2,3},{3,2},{4,5},{5,4},{6,7},{7,6},{8,9},{9,8},{10,11... | collective-permute-start | bytes 6291464 | tf_op jit(solution)/shard_map/ppermute | solution.py:733
  18.6 18.6 %all_to_all.15.table = f32[16,5,128]{2,1,0:T(8,128)S(1)} all-to-all(f32[16,5,128]{2,1,0:T(8,128)S(1)} %get-tuple-element.21), channel_id=1, replica_groups={{0,2,4,6,8,10,12,14,16,18,20,22,24,26,28,30},{1,3,5,7,9,11,13,15,17,19,..., dimensions={0} | all-to-all | bytes 81920 | tf_op jit(solution)/shard_map/all_to_all | solution.py:726
  37.2 5.0 %shard_map.120 = (s32[16]{0:T(128)S(1)}, bf16[4,576,128]{2,1,0:T(8,128)(2,1)S(1)}, bf16[4,576,128]{2,1,0:T(8,128)(2,1)S(1)}, bf16[4,768,128]{2,1,0:T(8,128)(2,1)S(1)}, bf16[4,384,128]{2,1,0:T(8,128)(2,1)S(1)}) custom-call(s32[2]{0:T(128)S(1)} %pad_add_fusion.place, bf16[128,4096]{1,0:T(8,128)(2,1)} %q_ref.7, bf16[128,4096]{1,0:T(8,128)(2,1)} %k_ref.7, ...), custom_call_target="tpu_custom_call" | custom-call | tf_op jit(solution)/shard_map/pallas_call | solution.py:281
  42.2 1.3 collective-permute-start.5
  43.5 0.7 collective-permute-start.4
  44.2 3.2 %collective-permute-start.2 = (bf16[4,576,128]{2,1,0:T(8,128)(2,1)S(1)}, bf16[4,576,128]{2,1,0:T(8,128)(2,1)S(1)}, u32[]{:S(2)}, u32[]{:S(2)}) collective-permute-start(bf16[4,576,128]{2,1,0:T(8,128)(2,1)S(1)} %get-tuple-element.25), channel_id=1, source_target_pairs={{0,2},{1,3},{4,6},{5,7},{8,10},{9,11},{12,14},{13,15},{16,18},{17,... | collective-permute-start | bytes 1769480 | tf_op jit(solution)/shard_map/ppermute | solution.py:698
  47.4 0.1 collective-permute-start.3
  47.5 6.9 %collective-permute-done.5.refs_3_ = bf16[4,384,128]{2,1,0:T(8,128)(2,1)S(1)} collective-permute-done((bf16[4,384,128]{2,1,0:T(8,128)(2,1)S(1)}, bf16[4,384,128]{2,1,0:T(8,128)(2,1)S(1)}, u32[]{:S(2)}, u32[]{:S(2)}) %collective-permute-start.5) | collective-permute-done | bytes 393248 | tf_op jit(solution)/shard_map/ppermute | solution.py:698
  54.4 19.7 %collective-permute-start.6 = (bf16[4,384,128]{2,1,0:T(8,128)(2,1)S(1)}, bf16[4,384,128]{2,1,0:T(8,128)(2,1)S(1)}, u32[]{:S(2)}, u32[]{:S(2)}) collective-permute-start(bf16[4,384,128]{2,1,0:T(8,128)(2,1)S(1)} %collective-permute-done.5.refs_3_), channel_id=1, source_target_pairs={{0,8},{1,9},{8,16},{9,17},{16,24},{17,25},{14,6},{15,7},{22,14},{2... | collective-permute-start | bytes 1179656 | tf_op jit(solution)/shard_map/ppermute | solution.py:698
  74.2 9.2 %shard_map.121 = (bf16[2,3,128,2048]{3,2,1,0:T(8,128)(2,1)S(1)}, f32[16,2,128]{2,1,0:T(2,128)S(1)}) custom-call(s32[16]{0:T(128)S(1)} %get-tuple-element.22.meta, bf16[128,4096]{1,0:T(8,128)(2,1)} %q_ref.7, bf16[128,4096]{1,0:T(8,128)(2,1)} %k_ref.7, bf16[128,4096]{1,0:T(8,128)(2,1)} %v_ref.7, bf16[128,4096]{1,0:T(8,128)(2,1)} %d_ref.7, ...), custom_call_target="tpu_custom_call" | custom-call | tf_op jit(solution)/shard_map/pallas_call | solution.py:429
  83.4 0.0 collective-permute-done.3.refs_1_
  83.4 5.0 %shard_map.122 = (bf16[2,3,128,2048]{3,2,1,0:T(8,128)(2,1)S(1)}, f32[16,2,128]{2,1,0:T(2,128)S(1)}, bf16[3,576,128]{2,1,0:T(8,128)(2,1)S(1)}, bf16[3,576,128]{2,...) custom-call(s32[16]{0:T(128)S(1)} %get-tuple-element.22.meta, ...), custom_call_target="tpu_custom_call" | custom-call | tf_op jit(solution)/shard_map/pallas_call | solution.py:548
  88.4 1.3 collective-permute-start.10
  89.7 0.7 collective-permute-start.9
  90.4 3.5 %collective-permute-start.7 = (bf16[3,576,128]{2,1,0:T(8,128)(2,1)S(1)}, bf16[3,576,128]{2,1,0:T(8,128)(2,1)S(1)}, u32[]{:S(2)}, u32[]{:S(2)}) collective-permute-start(bf16[3,576,128]{2,1,0:T(8,128)(2,1)S(1)} %get-tuple-element.30), channel_id=1, source_target_pairs={{0,2},{1,3},{4,6},{5,7},{8,10},{9,11},{12,14},{13,15},{16,18},{17,... | collective-permute-start | bytes 1327112 | tf_op jit(solution)/shard_map/ppermute | solution.py:698
  93.9 0.1 collective-permute-start.8
  94.0 10.5 %collective-permute-done.10.refs_3_ = bf16[3,384,128]{2,1,0:T(8,128)(2,1)S(1)} collective-permute-done((bf16[3,384,128]{2,1,0:T(8,128)(2,1)S(1)}, bf16[3,384,128]{2,1,0:T(8,128)(2,1)S(1)}, u32[]{:S(2)}, u32[]{:S(2)}) %collective-permute-start.10) | collective-permute-done | bytes 294944 | tf_op jit(solution)/shard_map/ppermute | solution.py:698
  104.5 10.4 %collective-permute-start.11 = (bf16[3,384,128]{2,1,0:T(8,128)(2,1)S(1)}, bf16[3,384,128]{2,1,0:T(8,128)(2,1)S(1)}, u32[]{:S(2)}, u32[]{:S(2)}) collective-permute-start(bf16[3,384,128]{2,1,0:T(8,128)(2,1)S(1)} %collective-permute-done.10.refs_3_), channel_id=1, source_target_pairs={{0,8},{1,9},{8,16},{9,17},{16,24},{17,25},{14,6},{15,7},{22,14},{2... | collective-permute-start | bytes 884744 | tf_op jit(solution)/shard_map/ppermute | solution.py:698
  115.0 22.0 %all_to_all.16.refs_5_ = f32[128,2,128]{2,1,0:T(2,128)S(1)} all-to-all(f32[128,2,128]{2,1,0:T(2,128)S(1)} %bitcast.5), channel_id=1, replica_groups={{0,2,4,6,8,10,12,14,16,18,20,22,24,26,28,30,32,34,36,38,40,42,44,46,48,..., dimensions={0} | all-to-all | bytes 262144 | tf_op jit(solution)/shard_map/all_to_all | solution.py:726
  137.0 1.6 %shard_map.123 = bf16[3,128,2048]{2,1,0:T(8,128)(2,1)S(1)} custom-call(s32[16]{0:T(128)S(1)} %get-tuple-element.22.meta, bf16[2,3,128,2048]{3,2,1,0:T(8,128)(2,1)S(1)} %get-tuple-element.29.in_ref, bf16[3,576,128]{2,1,0:T(8,128)(2,1)S(1)} %collective-permute-done.7.refs_0_, bf16[3,576,128]{2,1,0:T(8,128)(2,1)S(1)} %collective-permute-done.8.refs_1_, ...), custom_call_target="tpu_custom_call" | custom-call | tf_op jit(solution)/shard_map/pallas_call | solution.py:625
  138.7 5.1 %collective-permute-start.12 = (bf16[3,128,2048]{2,1,0:T(8,128)(2,1)S(1)}, bf16[3,128,2048]{2,1,0:T(8,128)(2,1)S(1)}, u32[]{:S(2)}, u32[]{:S(2)}) collective-permute-start(bf16[3,128,2048]{2,1,0:T(8,128)(2,1)S(1)} %shard_map.123), channel_id=1, source_target_pairs={{0,1},{1,0},{2,3},{3,2},{4,5},{5,4},{6,7},{7,6},{8,9},{9,8},{10,11... | collective-permute-start | bytes 4718600 | tf_op jit(solution)/shard_map/ppermute | solution.py:747
  143.8 3.0 %collective-permute-done.12.rec_ref = bf16[3,128,2048]{2,1,0:T(8,128)(2,1)S(1)} collective-permute-done((bf16[3,128,2048]{2,1,0:T(8,128)(2,1)S(1)}, bf16[3,128,2048]{2,1,0:T(8,128)(2,1)S(1)}, u32[]{:S(2)}, u32[]{:S(2)}) %collective-permute-start.12) | collective-permute-done | bytes 1572896 | tf_op jit(solution)/shard_map/ppermute | solution.py:747
  146.8 3.6 %shard_map.124 = (bf16[128,4096]{1,0:T(8,128)(2,1)}, bf16[128,4096]{1,0:T(8,128)(2,1)}, bf16[128,4096]{1,0:T(8,128)(2,1)}, f32[1,128]{1,0:T(1,128)}, f32[1,128]{1,0:T(1,128)}) custom-call(s32[16]{0:T(128)S(1)} %get-tuple-element.22.meta, bf16[2,3,128,2048]{3,2,1,0:T(8,128)(2,1)S(1)} %get-tuple-element.29.in_ref, ...), custom_call_target="tpu_custom_call" | custom-call | tf_op jit(solution)/shard_map/pallas_call | solution.py:663
  (9 shorter events, 0.1 us)
Async XLA Ops:
  1.9 11.4 %all-to-all-start = ((f32[8,2,16]{2,1,0:T(2,128)}), f32[8,2,16]{2,1,0:T(2,128)S(1)}, u32[]{:S(2)}, u32[]{:S(2)}) async-start(f32[8,2,16]{2,1,0:T(2,128)} %broadcast_in_dim.6), calls=%async_computation | async-start | bytes 16384 | tf_op jit(solution)/shard_map/all_to_all | solution.py:726
  9.6 1.8 %collective-permute-start = (f32[2,128]{1,0:T(2,128)S(1)}, f32[2,128]{1,0:T(2,128)S(1)}, u32[]{:S(2)}, u32[]{:S(2)}) collective-permute-start(f32[2,128]{1,0:T(2,128)S(1)} %pad_convert_fusion.info), channel_id=1, source_target_pairs={{0,1},{1,0},{2,3},{3,2},{4,5},{5,4},{6,7},{7,6},{8,9},{9,8},{10,11... | collective-permute-start | bytes 3080 | tf_op jit(solution)/shard_map/ppermute | solution.py:729
  16.4 20.8 %collective-permute-start.1 = (bf16[4,128,2048]{2,1,0:T(8,128)(2,1)S(1)}, bf16[4,128,2048]{2,1,0:T(8,128)(2,1)S(1)}, u32[]{:S(2)}, u32[]{:S(2)}) collective-permute-start(bf16[4,128,2048]{2,1,0:T(8,128)(2,1)S(1)} %get-tuple-element.20), channel_id=1, source_target_pairs={{0,1},{1,0},{2,3},{3,2},{4,5},{5,4},{6,7},{7,6},{8,9},{9,8},{10,11... | collective-permute-start | bytes 6291464 | tf_op jit(solution)/shard_map/ppermute | solution.py:733
  42.2 12.2 %collective-permute-start.5 = (bf16[4,384,128]{2,1,0:T(8,128)(2,1)S(1)}, bf16[4,384,128]{2,1,0:T(8,128)(2,1)S(1)}, u32[]{:S(2)}, u32[]{:S(2)}) collective-permute-start(bf16[4,384,128]{2,1,0:T(8,128)(2,1)S(1)} %get-tuple-element.28), channel_id=1, source_target_pairs={{2,4},{3,5},{10,12},{11,13},{18,20},{19,21},{26,28},{27,29},{4,2},... | collective-permute-start | bytes 1179656 | tf_op jit(solution)/shard_map/ppermute | solution.py:698
  43.5 39.9 %collective-permute-start.4 = (bf16[4,768,128]{2,1,0:T(8,128)(2,1)S(1)}, bf16[4,768,128]{2,1,0:T(8,128)(2,1)S(1)}, u32[]{:S(2)}, u32[]{:S(2)}) collective-permute-start(bf16[4,768,128]{2,1,0:T(8,128)(2,1)S(1)} %get-tuple-element.27), channel_id=1, source_target_pairs={{2,4},{3,5},{6,8},{7,9},{10,12},{11,13},{14,16},{15,17},{18,20},{1... | collective-permute-start | bytes 2359304 | tf_op jit(solution)/shard_map/ppermute | solution.py:698
  44.2 39.2 %collective-permute-start.2 = (bf16[4,576,128]{2,1,0:T(8,128)(2,1)S(1)}, bf16[4,576,128]{2,1,0:T(8,128)(2,1)S(1)}, u32[]{:S(2)}, u32[]{:S(2)}) collective-permute-start(bf16[4,576,128]{2,1,0:T(8,128)(2,1)S(1)} %get-tuple-element.25), channel_id=1, source_target_pairs={{0,2},{1,3},{4,6},{5,7},{8,10},{9,11},{12,14},{13,15},{16,18},{17,... | collective-permute-start | bytes 1769480 | tf_op jit(solution)/shard_map/ppermute | solution.py:698
  47.4 36.0 %collective-permute-start.3 = (bf16[4,576,128]{2,1,0:T(8,128)(2,1)S(1)}, bf16[4,576,128]{2,1,0:T(8,128)(2,1)S(1)}, u32[]{:S(2)}, u32[]{:S(2)}) collective-permute-start(bf16[4,576,128]{2,1,0:T(8,128)(2,1)S(1)} %get-tuple-element.26), channel_id=1, source_target_pairs={{0,2},{1,3},{4,6},{5,7},{8,10},{9,11},{12,14},{13,15},{16,18},{17,... | collective-permute-start | bytes 1769480 | tf_op jit(solution)/shard_map/ppermute | solution.py:698
  54.4 28.9 %collective-permute-start.6 = (bf16[4,384,128]{2,1,0:T(8,128)(2,1)S(1)}, bf16[4,384,128]{2,1,0:T(8,128)(2,1)S(1)}, u32[]{:S(2)}, u32[]{:S(2)}) collective-permute-start(bf16[4,384,128]{2,1,0:T(8,128)(2,1)S(1)} %collective-permute-done.5.refs_3_), channel_id=1, source_target_pairs={{0,8},{1,9},{8,16},{9,17},{16,24},{17,25},{14,6},{15,7},{22,14},{2... | collective-permute-start | bytes 1179656 | tf_op jit(solution)/shard_map/ppermute | solution.py:698
  88.4 16.1 %collective-permute-start.10 = (bf16[3,384,128]{2,1,0:T(8,128)(2,1)S(1)}, bf16[3,384,128]{2,1,0:T(8,128)(2,1)S(1)}, u32[]{:S(2)}, u32[]{:S(2)}) collective-permute-start(bf16[3,384,128]{2,1,0:T(8,128)(2,1)S(1)} %get-tuple-element.33), channel_id=1, source_target_pairs={{2,4},{3,5},{10,12},{11,13},{18,20},{19,21},{26,28},{27,29},{4,2},... | collective-permute-start | bytes 884744 | tf_op jit(solution)/shard_map/ppermute | solution.py:698
  89.7 47.3 %collective-permute-start.9 = (bf16[3,768,128]{2,1,0:T(8,128)(2,1)S(1)}, bf16[3,768,128]{2,1,0:T(8,128)(2,1)S(1)}, u32[]{:S(2)}, u32[]{:S(2)}) collective-permute-start(bf16[3,768,128]{2,1,0:T(8,128)(2,1)S(1)} %get-tuple-element.32), channel_id=1, source_target_pairs={{2,4},{3,5},{6,8},{7,9},{10,12},{11,13},{14,16},{15,17},{18,20},{1... | collective-permute-start | bytes 1769480 | tf_op jit(solution)/shard_map/ppermute | solution.py:698
  90.4 46.5 %collective-permute-start.7 = (bf16[3,576,128]{2,1,0:T(8,128)(2,1)S(1)}, bf16[3,576,128]{2,1,0:T(8,128)(2,1)S(1)}, u32[]{:S(2)}, u32[]{:S(2)}) collective-permute-start(bf16[3,576,128]{2,1,0:T(8,128)(2,1)S(1)} %get-tuple-element.30), channel_id=1, source_target_pairs={{0,2},{1,3},{4,6},{5,7},{8,10},{9,11},{12,14},{13,15},{16,18},{17,... | collective-permute-start | bytes 1327112 | tf_op jit(solution)/shard_map/ppermute | solution.py:698
  93.9 43.1 %collective-permute-start.8 = (bf16[3,576,128]{2,1,0:T(8,128)(2,1)S(1)}, bf16[3,576,128]{2,1,0:T(8,128)(2,1)S(1)}, u32[]{:S(2)}, u32[]{:S(2)}) collective-permute-start(bf16[3,576,128]{2,1,0:T(8,128)(2,1)S(1)} %get-tuple-element.31), channel_id=1, source_target_pairs={{0,2},{1,3},{4,6},{5,7},{8,10},{9,11},{12,14},{13,15},{16,18},{17,... | collective-permute-start | bytes 1327112 | tf_op jit(solution)/shard_map/ppermute | solution.py:698
  104.5 32.5 %collective-permute-start.11 = (bf16[3,384,128]{2,1,0:T(8,128)(2,1)S(1)}, bf16[3,384,128]{2,1,0:T(8,128)(2,1)S(1)}, u32[]{:S(2)}, u32[]{:S(2)}) collective-permute-start(bf16[3,384,128]{2,1,0:T(8,128)(2,1)S(1)} %collective-permute-done.10.refs_3_), channel_id=1, source_target_pairs={{0,8},{1,9},{8,16},{9,17},{16,24},{17,25},{14,6},{15,7},{22,14},{2... | collective-permute-start | bytes 884744 | tf_op jit(solution)/shard_map/ppermute | solution.py:698
  138.7 8.1 %collective-permute-start.12 = (bf16[3,128,2048]{2,1,0:T(8,128)(2,1)S(1)}, bf16[3,128,2048]{2,1,0:T(8,128)(2,1)S(1)}, u32[]{:S(2)}, u32[]{:S(2)}) collective-permute-start(bf16[3,128,2048]{2,1,0:T(8,128)(2,1)S(1)} %shard_map.123), channel_id=1, source_target_pairs={{0,1},{1,0},{2,3},{3,2},{4,5},{5,4},{6,7},{7,6},{8,9},{9,8},{10,11... | collective-permute-start | bytes 4718600 | tf_op jit(solution)/shard_map/ppermute | solution.py:747
where the time goes:
time: 152 us; the launch traced here: 151 us
  starting transfers between devices  55.6 us (37%)
  blocking collectives  40.6 us (27%)
  Pallas kernels  27.5 us (18%)
  waiting for transfers between devices  23.2 us (15%)
  between operations  1.59 us (1%)
    ppermute x10, starting transfers between devices, move(): return lax.ppermute(array, 'seq', pairs)  41 us
    all_to_all x2, blocking collectives, all_to_all(): lax.all_to_all(array, axis, 0, 0, axis_index_groups=among, tiled=True)  40.6 us
    ppermute x10, waiting for transfers between devices, move(): return lax.ppermute(array, 'seq', pairs)  17.4 us
    pallas_call x1, Pallas kernels, solve_mid(): pl.pallas_call(mid_kernel, out_shape=(jax.ShapeDtypeStruct((2, 3, ROWS, H...  9.21 us
    all_to_all x1, starting transfers between devices, all_to_all(): lax.all_to_all(array, axis, 0, 0, axis_index_groups=among, tiled=True)  6.37 us
    ppermute x1, starting transfers between devices, shards(): other = lax.ppermute(send, 'seq', swap)  5.11 us
    pallas_call x1, Pallas kernels, solve_edges(): pl.pallas_call(edge_kernel, out_shape=(jax.ShapeDtypeStruct(mid.shape, BF...  5.02 us
    pallas_call x1, Pallas kernels, pack_halos(): pl.pallas_call(pack_kernel, out_shape=(jax.ShapeDtypeStruct((16,), jnp.in...  4.96 us
  transfers between devices with their start and end apart: 14, of which 5 were waited for; matrix products, arithmetic and copies ran while one was open for 1% of the time, Pallas kernels for 6%

commit v1 on v0

--- a/solution.py
+++ b/solution.py
@@ -16,7 +16,7 @@
 ALIGN = 16
 LINE = 4
 CAP = 1152
-PARTS = (CAP // 2,) * 2
+PARTS = (CAP,)
 FIRST = 768
 REST = CAP - FIRST
 SENT = len(PARTS) + 2

time: 152 us -> 154 us (1.013); the launches traced: 151 us -> 154 us
  waiting for transfers between devices: 23.2 us -> 30.7 us
  starting transfers between devices: 55.6 us -> 49.7 us
  blocking collectives: 40.6 us -> 43 us
    ppermute x10 -> x8, starting transfers between devices: 41 us -> 30.9 us  [move(): return lax.ppermute(array, 'seq', pairs)]
    ppermute x10 -> x8, waiting for transfers between devices: 17.4 us -> 25 us  [move(): return lax.ppermute(array, 'seq', pairs)]
    ppermute x1, starting transfers between devices: 5.11 us -> 9.27 us  [shards(): other = lax.ppermute(send, 'seq', swap)]
    all_to_all x2, blocking collectives: 40.6 us -> 43 us  [all_to_all(): lax.all_to_all(array, axis, 0, 0, axis_index_groups=among, tiled=True)]
  transfers between devices with their start and end apart: 14 -> 12, of which waited for: 5 -> 5; matrix products, arithmetic and copies ran while one was open for 1% -> 1% of each run, Pallas kernels for 6% -> 6%
where the time goes in v1:
time: 154 us
  starting transfers between devices  49.7 us (32%)
  blocking collectives  43 us (28%)
  waiting for transfers between devices  30.7 us (20%)
  Pallas kernels  27.1 us (18%)
  between operations  1.59 us (1%)
    all_to_all x2, blocking collectives, all_to_all(): lax.all_to_all(array, axis, 0, 0, axis_index_groups=among, tiled=True)  43 us
    ppermute x8, starting transfers between devices, move(): return lax.ppermute(array, 'seq', pairs)  30.9 us
    ppermute x8, waiting for transfers between devices, move(): return lax.ppermute(array, 'seq', pairs)  25 us
    ppermute x1, starting transfers between devices, shards(): other = lax.ppermute(send, 'seq', swap)  9.27 us
    pallas_call x1, Pallas kernels, solve_mid(): pl.pallas_call(mid_kernel, out_shape=(jax.ShapeDtypeStruct((2, 3, ROWS, H...  9.22 us
    all_to_all x1, starting transfers between devices, all_to_all(): lax.all_to_all(array, axis, 0, 0, axis_index_groups=among, tiled=True)  6.37 us
    pallas_call x1, Pallas kernels, pack_halos(): pl.pallas_call(pack_kernel, out_shape=(jax.ShapeDtypeStruct((16,), jnp.in...  4.95 us
    pallas_call x1, Pallas kernels, solve_edges(): pl.pallas_call(edge_kernel, out_shape=(jax.ShapeDtypeStruct(mid.shape, BF...  4.87 us
  transfers between devices with their start and end apart: 12, of which 5 were waited for; matrix products, arithmetic and copies ran while one was open for 1% of the time, Pallas kernels for 6%

profile of v1, /device:TPU:1, one launch (start us, length us, event | category | flops | bytes accessed | tf_op | source)
XLA Modules:
  0.0 154.2 jit_solution(9533450418764961270)
XLA Ops:
  0.6 0.7 pad_maximum_fusion
  1.3 0.6 broadcast_in_dim.6
  1.9 6.4 %all-to-all-start = ((f32[8,2,16]{2,1,0:T(2,128)}), f32[8,2,16]{2,1,0:T(2,128)S(1)}, u32[]{:S(2)}, u32[]{:S(2)}) async-start(f32[8,2,16]{2,1,0:T(2,128)} %broadcast_in_dim.6), calls=%async_computation | async-start | bytes 16384 | tf_op jit(solution)/shard_map/all_to_all | solution.py:726
  8.9 0.7 pad_convert_fusion.info
  9.6 1.0 collective-permute-start
  10.6 0.1 pad_add_fusion.place
  10.6 0.7 collective-permute-done.info_other
  11.4 1.9 %all-to-all-done.gain_cols = f32[8,2,16]{2,1,0:T(2,128)S(1)} async-done(((f32[8,2,16]{2,1,0:T(2,128)}), f32[8,2,16]{2,1,0:T(2,128)S(1)}, u32[]{:S(2)}, u32[]{:S(2)}) %all-to-all-start) | async-done | bytes 1056 | tf_op jit(solution)/shard_map/all_to_all | solution.py:726
  13.3 3.1 %shard_map.119 = (bf16[4,128,2048]{2,1,0:T(8,128)(2,1)S(1)}, f32[16,5,128]{2,1,0:T(8,128)S(1)}) custom-call(s32[2]{0:T(128)S(1)} %pad_add_fusion.place, bf16[128,4096]{1,0:T(8,128)(2,1)} %q_ref.7, bf16[128,4096]{1,0:T(8,128)(2,1)} %k_ref.7, bf16[128,4096]{1,0:T(8,128)(2,1)} %v_ref.7, bf16[128,4096]{1,0:T(8,128)(2,1)} %d_ref.7, ...), custom_call_target="tpu_custom_call" | custom-call | tf_op jit(solution)/shard_map/pallas_call | solution.py:87
  16.4 2.2 %collective-permute-start.1 = (bf16[4,128,2048]{2,1,0:T(8,128)(2,1)S(1)}, bf16[4,128,2048]{2,1,0:T(8,128)(2,1)S(1)}, u32[]{:S(2)}, u32[]{:S(2)}) collective-permute-start(bf16[4,128,2048]{2,1,0:T(8,128)(2,1)S(1)} %get-tuple-element.18), channel_id=1, source_target_pairs={{0,1},{1,0},{2,3},{3,2},{4,5},{5,4},{6,7},{7,6},{8,9},{9,8},{10,11... | collective-permute-start | bytes 6291464 | tf_op jit(solution)/shard_map/ppermute | solution.py:733
  18.6 18.6 %all_to_all.15.table = f32[16,5,128]{2,1,0:T(8,128)S(1)} all-to-all(f32[16,5,128]{2,1,0:T(8,128)S(1)} %get-tuple-element.19), channel_id=1, replica_groups={{0,2,4,6,8,10,12,14,16,18,20,22,24,26,28,30},{1,3,5,7,9,11,13,15,17,19,..., dimensions={0} | all-to-all | bytes 81920 | tf_op jit(solution)/shard_map/all_to_all | solution.py:726
  37.2 0.0 collective-permute-done.1.rec_ref
  37.2 4.9 %shard_map.120 = (s32[16]{0:T(128)S(1)}, bf16[4,1152,128]{2,1,0:T(8,128)(2,1)S(1)}, bf16[4,768,128]{2,1,0:T(8,128)(2,1)S(1)}, bf16[4,384,128]{2,1,0:T(8,128)(2,1)S(1)}) custom-call(s32[2]{0:T(128)S(1)} %pad_add_fusion.place, bf16[128,4096]{1,0:T(8,128)(2,1)} %q_ref.7, bf16[128,4096]{1,0:T(8,128)(2,1)} %k_ref.7, bf16[128,4096]{1,0:T(8,128)(2,1)} %v_ref.7, ...), custom_call_target="tpu_custom_call" | custom-call | tf_op jit(solution)/shard_map/pallas_call | solution.py:281
  42.2 0.1 collective-permute-start.2
  42.3 1.3 collective-permute-start.4
  43.6 0.7 collective-permute-start.3
  44.3 10.1 %collective-permute-done.4.refs_2_ = bf16[4,384,128]{2,1,0:T(8,128)(2,1)S(1)} collective-permute-done((bf16[4,384,128]{2,1,0:T(8,128)(2,1)S(1)}, bf16[4,384,128]{2,1,0:T(8,128)(2,1)S(1)}, u32[]{:S(2)}, u32[]{:S(2)}) %collective-permute-start.4) | collective-permute-done | bytes 393248 | tf_op jit(solution)/shard_map/ppermute | solution.py:698
  54.4 19.6 %collective-permute-start.5 = (bf16[4,384,128]{2,1,0:T(8,128)(2,1)S(1)}, bf16[4,384,128]{2,1,0:T(8,128)(2,1)S(1)}, u32[]{:S(2)}, u32[]{:S(2)}) collective-permute-start(bf16[4,384,128]{2,1,0:T(8,128)(2,1)S(1)} %collective-permute-done.4.refs_2_), channel_id=1, source_target_pairs={{0,8},{1,9},{8,16},{9,17},{16,24},{17,25},{14,6},{15,7},{22,14},{2... | collective-permute-start | bytes 1179656 | tf_op jit(solution)/shard_map/ppermute | solution.py:698
  74.1 9.2 %shard_map.121 = (bf16[2,3,128,2048]{3,2,1,0:T(8,128)(2,1)S(1)}, f32[16,2,128]{2,1,0:T(2,128)S(1)}) custom-call(s32[16]{0:T(128)S(1)} %get-tuple-element.20.meta, bf16[128,4096]{1,0:T(8,128)(2,1)} %q_ref.7, bf16[128,4096]{1,0:T(8,128)(2,1)} %k_ref.7, bf16[128,4096]{1,0:T(8,128)(2,1)} %v_ref.7, bf16[128,4096]{1,0:T(8,128)(2,1)} %d_ref.7, ...), custom_call_target="tpu_custom_call" | custom-call | tf_op jit(solution)/shard_map/pallas_call | solution.py:429
  83.3 0.0 collective-permute-done.5.refs_3_
  83.3 0.0 collective-permute-done.3.refs_1_
  83.3 4.9 %shard_map.122 = (bf16[2,3,128,2048]{3,2,1,0:T(8,128)(2,1)S(1)}, f32[16,2,128]{2,1,0:T(2,128)S(1)}, bf16[3,1152,128]{2,1,0:T(8,128)(2,1)S(1)}, bf16[3,768,128]{2,1,0:T(8,128)(2,1)S(1)}, bf16[3,384,128]{2,1,0:T(8,128)(2,1)S(1)}) custom-call(s32[16]{0:T(128)S(1)} %get-tuple-element.20.meta, bf16[128,4096]{1,0:T(8,128)(2,1)} %q_ref.7, bf16[128,4096]{1,0:T(8,128)(2,1)} %k_ref.7, ...), custom_call_target="tpu_custom_call" | custom-call | tf_op jit(solution)/shard_map/pallas_call | solution.py:548
  88.2 0.1 collective-permute-start.6
  88.3 1.3 collective-permute-start.8
  89.6 0.7 collective-permute-start.7
  90.3 14.8 %collective-permute-done.8.refs_2_ = bf16[3,384,128]{2,1,0:T(8,128)(2,1)S(1)} collective-permute-done((bf16[3,384,128]{2,1,0:T(8,128)(2,1)S(1)}, bf16[3,384,128]{2,1,0:T(8,128)(2,1)S(1)}, u32[]{:S(2)}, u32[]{:S(2)}) %collective-permute-start.8) | collective-permute-done | bytes 294944 | tf_op jit(solution)/shard_map/ppermute | solution.py:698
  105.1 7.1 %collective-permute-start.9 = (bf16[3,384,128]{2,1,0:T(8,128)(2,1)S(1)}, bf16[3,384,128]{2,1,0:T(8,128)(2,1)S(1)}, u32[]{:S(2)}, u32[]{:S(2)}) collective-permute-start(bf16[3,384,128]{2,1,0:T(8,128)(2,1)S(1)} %collective-permute-done.8.refs_2_), channel_id=1, source_target_pairs={{0,8},{1,9},{8,16},{9,17},{16,24},{17,25},{14,6},{15,7},{22,14},{2... | collective-permute-start | bytes 884744 | tf_op jit(solution)/shard_map/ppermute | solution.py:698
  112.3 24.4 %all_to_all.16.refs_4_ = f32[128,2,128]{2,1,0:T(2,128)S(1)} all-to-all(f32[128,2,128]{2,1,0:T(2,128)S(1)} %bitcast.5), channel_id=1, replica_groups={{0,2,4,6,8,10,12,14,16,18,20,22,24,26,28,30,32,34,36,38,40,42,44,46,48,..., dimensions={0} | all-to-all | bytes 262144 | tf_op jit(solution)/shard_map/all_to_all | solution.py:726
  136.7 1.5 shard_map.123
  138.3 9.3 %collective-permute-start.10 = (bf16[3,128,2048]{2,1,0:T(8,128)(2,1)S(1)}, bf16[3,128,2048]{2,1,0:T(8,128)(2,1)S(1)}, u32[]{:S(2)}, u32[]{:S(2)}) collective-permute-start(bf16[3,128,2048]{2,1,0:T(8,128)(2,1)S(1)} %shard_map.123), channel_id=1, source_target_pairs={{0,1},{1,0},{2,3},{3,2},{4,5},{5,4},{6,7},{7,6},{8,9},{9,8},{10,11... | collective-permute-start | bytes 4718600 | tf_op jit(solution)/shard_map/ppermute | solution.py:747
  147.5 3.0 %collective-permute-done.10.rec_ref = bf16[3,128,2048]{2,1,0:T(8,128)(2,1)S(1)} collective-permute-done((bf16[3,128,2048]{2,1,0:T(8,128)(2,1)S(1)}, bf16[3,128,2048]{2,1,0:T(8,128)(2,1)S(1)}, u32[]{:S(2)}, u32[]{:S(2)}) %collective-permute-start.10) | collective-permute-done | bytes 1572896 | tf_op jit(solution)/shard_map/ppermute | solution.py:747
  150.6 3.4 %shard_map.124 = (bf16[128,4096]{1,0:T(8,128)(2,1)}, bf16[128,4096]{1,0:T(8,128)(2,1)}, bf16[128,4096]{1,0:T(8,128)(2,1)}, f32[1,128]{1,0:T(1,128)}, f32[1,128]{1,0:T(1,128)}) custom-call(s32[16]{0:T(128)S(1)} %get-tuple-element.20.meta, bf16[2,3,128,2048]{3,2,1,0:T(8,128)(2,1)S(1)} %get-tuple-element.26.in_ref, ...), custom_call_target="tpu_custom_call" | custom-call | tf_op jit(solution)/shard_map/pallas_call | solution.py:663
  (5 shorter events, 0.0 us)
Async XLA Ops:
  1.9 11.4 %all-to-all-start = ((f32[8,2,16]{2,1,0:T(2,128)}), f32[8,2,16]{2,1,0:T(2,128)S(1)}, u32[]{:S(2)}, u32[]{:S(2)}) async-start(f32[8,2,16]{2,1,0:T(2,128)} %broadcast_in_dim.6), calls=%async_computation | async-start | bytes 16384 | tf_op jit(solution)/shard_map/all_to_all | solution.py:726
  9.6 1.8 %collective-permute-start = (f32[2,128]{1,0:T(2,128)S(1)}, f32[2,128]{1,0:T(2,128)S(1)}, u32[]{:S(2)}, u32[]{:S(2)}) collective-permute-start(f32[2,128]{1,0:T(2,128)S(1)} %pad_convert_fusion.info), channel_id=1, source_target_pairs={{0,1},{1,0},{2,3},{3,2},{4,5},{5,4},{6,7},{7,6},{8,9},{9,8},{10,11... | collective-permute-start | bytes 3080 | tf_op jit(solution)/shard_map/ppermute | solution.py:729
  16.4 20.8 %collective-permute-start.1 = (bf16[4,128,2048]{2,1,0:T(8,128)(2,1)S(1)}, bf16[4,128,2048]{2,1,0:T(8,128)(2,1)S(1)}, u32[]{:S(2)}, u32[]{:S(2)}) collective-permute-start(bf16[4,128,2048]{2,1,0:T(8,128)(2,1)S(1)} %get-tuple-element.18), channel_id=1, source_target_pairs={{0,1},{1,0},{2,3},{3,2},{4,5},{5,4},{6,7},{7,6},{8,9},{9,8},{10,11... | collective-permute-start | bytes 6291464 | tf_op jit(solution)/shard_map/ppermute | solution.py:733
  42.2 41.1 %collective-permute-start.2 = (bf16[4,1152,128]{2,1,0:T(8,128)(2,1)S(1)}, bf16[4,1152,128]{2,1,0:T(8,128)(2,1)S(1)}, u32[]{:S(2)}, u32[]{:S(2)}) collective-permute-start(bf16[4,1152,128]{2,1,0:T(8,128)(2,1)S(1)} %get-tuple-element.23), channel_id=1, source_target_pairs={{0,2},{1,3},{4,6},{5,7},{8,10},{9,11},{12,14},{13,15},{16,18},{17,... | collective-permute-start | bytes 3538952 | tf_op jit(solution)/shard_map/ppermute | solution.py:698
  42.3 12.1 %collective-permute-start.4 = (bf16[4,384,128]{2,1,0:T(8,128)(2,1)S(1)}, bf16[4,384,128]{2,1,0:T(8,128)(2,1)S(1)}, u32[]{:S(2)}, u32[]{:S(2)}) collective-permute-start(bf16[4,384,128]{2,1,0:T(8,128)(2,1)S(1)} %get-tuple-element.25), channel_id=1, source_target_pairs={{2,4},{3,5},{10,12},{11,13},{18,20},{19,21},{26,28},{27,29},{4,2},... | collective-permute-start | bytes 1179656 | tf_op jit(solution)/shard_map/ppermute | solution.py:698
  43.6 39.7 %collective-permute-start.3 = (bf16[4,768,128]{2,1,0:T(8,128)(2,1)S(1)}, bf16[4,768,128]{2,1,0:T(8,128)(2,1)S(1)}, u32[]{:S(2)}, u32[]{:S(2)}) collective-permute-start(bf16[4,768,128]{2,1,0:T(8,128)(2,1)S(1)} %get-tuple-element.24), channel_id=1, source_target_pairs={{2,4},{3,5},{6,8},{7,9},{10,12},{11,13},{14,16},{15,17},{18,20},{1... | collective-permute-start | bytes 2359304 | tf_op jit(solution)/shard_map/ppermute | solution.py:698
  54.4 28.9 %collective-permute-start.5 = (bf16[4,384,128]{2,1,0:T(8,128)(2,1)S(1)}, bf16[4,384,128]{2,1,0:T(8,128)(2,1)S(1)}, u32[]{:S(2)}, u32[]{:S(2)}) collective-permute-start(bf16[4,384,128]{2,1,0:T(8,128)(2,1)S(1)} %collective-permute-done.4.refs_2_), channel_id=1, source_target_pairs={{0,8},{1,9},{8,16},{9,17},{16,24},{17,25},{14,6},{15,7},{22,14},{2... | collective-permute-start | bytes 1179656 | tf_op jit(solution)/shard_map/ppermute | solution.py:698
  88.2 48.5 %collective-permute-start.6 = (bf16[3,1152,128]{2,1,0:T(8,128)(2,1)S(1)}, bf16[3,1152,128]{2,1,0:T(8,128)(2,1)S(1)}, u32[]{:S(2)}, u32[]{:S(2)}) collective-permute-start(bf16[3,1152,128]{2,1,0:T(8,128)(2,1)S(1)} %get-tuple-element.27), channel_id=1, source_target_pairs={{0,2},{1,3},{4,6},{5,7},{8,10},{9,11},{12,14},{13,15},{16,18},{17,... | collective-permute-start | bytes 2654216 | tf_op jit(solution)/shard_map/ppermute | solution.py:698
  88.3 16.8 %collective-permute-start.8 = (bf16[3,384,128]{2,1,0:T(8,128)(2,1)S(1)}, bf16[3,384,128]{2,1,0:T(8,128)(2,1)S(1)}, u32[]{:S(2)}, u32[]{:S(2)}) collective-permute-start(bf16[3,384,128]{2,1,0:T(8,128)(2,1)S(1)} %get-tuple-element.29), channel_id=1, source_target_pairs={{2,4},{3,5},{10,12},{11,13},{18,20},{19,21},{26,28},{27,29},{4,2},... | collective-permute-start | bytes 884744 | tf_op jit(solution)/shard_map/ppermute | solution.py:698
  89.6 47.1 %collective-permute-start.7 = (bf16[3,768,128]{2,1,0:T(8,128)(2,1)S(1)}, bf16[3,768,128]{2,1,0:T(8,128)(2,1)S(1)}, u32[]{:S(2)}, u32[]{:S(2)}) collective-permute-start(bf16[3,768,128]{2,1,0:T(8,128)(2,1)S(1)} %get-tuple-element.28), channel_id=1, source_target_pairs={{2,4},{3,5},{6,8},{7,9},{10,12},{11,13},{14,16},{15,17},{18,20},{1... | collective-permute-start | bytes 1769480 | tf_op jit(solution)/shard_map/ppermute | solution.py:698
  105.1 31.6 %collective-permute-start.9 = (bf16[3,384,128]{2,1,0:T(8,128)(2,1)S(1)}, bf16[3,384,128]{2,1,0:T(8,128)(2,1)S(1)}, u32[]{:S(2)}, u32[]{:S(2)}) collective-permute-start(bf16[3,384,128]{2,1,0:T(8,128)(2,1)S(1)} %collective-permute-done.8.refs_2_), channel_id=1, source_target_pairs={{0,8},{1,9},{8,16},{9,17},{16,24},{17,25},{14,6},{15,7},{22,14},{2... | collective-permute-start | bytes 884744 | tf_op jit(solution)/shard_map/ppermute | solution.py:698
  138.3 12.3 %collective-permute-start.10 = (bf16[3,128,2048]{2,1,0:T(8,128)(2,1)S(1)}, bf16[3,128,2048]{2,1,0:T(8,128)(2,1)S(1)}, u32[]{:S(2)}, u32[]{:S(2)}) collective-permute-start(bf16[3,128,2048]{2,1,0:T(8,128)(2,1)S(1)} %shard_map.123), channel_id=1, source_target_pairs={{0,1},{1,0},{2,3},{3,2},{4,5},{5,4},{6,7},{7,6},{8,9},{9,8},{10,11... | collective-permute-start | bytes 4718600 | tf_op jit(solution)/shard_map/ppermute | solution.py:747
